TPU v7x, 32 devices: a whole 2x2x4 slice. The times are simulated.
32 devices in a mesh: mem: 4 (over y, x), col: 8 (over z, core).
Axes of the slice: x: 2, y: 2, z: 4, core: 2. Of those that a mesh axis runs over, the one named last changes fastest.
Arguments:
- perturbations: bfloat16 [32, 32, 256, 128], P('mem', 'col'), may hold values from -4 to 4
- static_root: float32 [128, 128], replicated, may hold values from -0.5 to 1.5
- obs_jacobian: float32 [128, 128], replicated, may hold values from -0.5 to 0.5
- innovations: float32 [2048, 128], P('col'), may hold values from -6 to 6
- obs_weights: float32 [128], replicated, may hold values from 0.2 to 2
- length_scale: float32 [32, 256], P('col'), may hold values from 0.05 to 0.24
- obs_owner: int32 [2048, 1], P('col'), may hold values from 0 to 7; in each aligned block of 256 rows (0 to 255, 256 to 511, ...) at most 64 rows name the same one
- obs_cell: int32 [2048], P('col'), may hold values from 0 to 1023
- obs_count: int32 [8], P('col'), may hold values from 128 to 256, as said below
Outputs:
- increment: float32 [32, 256, 128], P('col', 'mem')
- control_static: float32 [32, 256, 128], P('col', 'mem')
- control_ensemble: float32 [32, 32, 256], P('mem', 'col')
Inputs may be any that keep to these rules, and one draw needn't show every extreme that they name: `obs_owner`: each holder's 256 rows name any one column block at most 64 times. `obs_count`: rows at or past a holder's count are padding and are ignored; at least one holder is full. `obs_cell`: the column within the owner's block, numbered y * 256 + x, where y is its grid row within the block (0 to 3).
All inputs are finite; a program needn't handle non-finite values.
Results may differ from a plain program's by a relative error of at most 0.004.
Values may be sent and summed in bfloat16 or wider, within the bound.
A program may use at most 64 MiB of HBM per device.

v0:
```python
import jax
import jax.numpy as jnp
from jax import lax
from jax.sharding import PartitionSpec as P

NSWEEP = 4
ITERS = 2


def extended(block, sides, width):
    for axis, dim in sides:
        count = lax.axis_size(axis)
        forward = [(i, i + 1) for i in range(count - 1)]
        backward = [(target, source) for source, target in forward]
        low = lax.ppermute(
            lax.slice_in_dim(block, block.shape[dim] - width, None, axis=dim), axis, forward
        )
        high = lax.ppermute(lax.slice_in_dim(block, 0, width, axis=dim), axis, backward)
        block = jnp.concatenate([low, block, high], axis=dim)
    return block


def face_coefficients(length_scale):
    rimmed = extended(length_scale, (("col", 0),), 1)
    padded = jnp.pad(rimmed, ((0, 0), (1, 1)))
    return (
        jnp.sqrt(length_scale * padded[:-2, 1:-1]),
        jnp.sqrt(length_scale * padded[2:, 1:-1]),
        jnp.sqrt(length_scale * padded[1:-1, :-2]),
        jnp.sqrt(length_scale * padded[1:-1, 2:]),
    )


def sweeps(values, coeffs):
    face_up, face_down, face_left, face_right = coeffs
    for sweep_step in range(NSWEEP):
        rimmed = extended(values, (("col", 1),), 1)
        padded = jnp.pad(rimmed, ((0, 0), (0, 0), (1, 1)))
        centre = values
        values = (
            centre
            + face_up * (padded[:, :-2, 1:-1] - centre)
            + face_down * (padded[:, 2:, 1:-1] - centre)
            + face_left * (padded[:, 1:-1, :-2] - centre)
            + face_right * (padded[:, 1:-1, 2:] - centre)
        )
    return values


def local_inner(first, second):
    return jnp.sum(first[0] * second[0]) + jnp.sum(first[1] * second[1])


def shards(
    perturbations,
    static_root,
    obs_jacobian,
    innovations,
    obs_weights,
    length_scale,
    obs_owner,
    obs_cell,
    obs_count,
):
    members, rows_here, columns, features = perturbations.shape
    quarter = columns // lax.axis_size("mem")
    offset = lax.axis_index("mem") * quarter
    blocks = lax.axis_size("col")
    obs_dev, channels = innovations.shape
    capacity = max(2, 2 * obs_dev // blocks)
    total_slots = blocks * capacity
    coeffs = face_coefficients(length_scale)
    is_live = jnp.arange(obs_dev, dtype=jnp.int32) < obs_count[0]
    owner_ids = obs_owner[:, 0]
    onehot = (
        (owner_ids[:, None] == jnp.arange(blocks, dtype=jnp.int32)[None, :]) & is_live[:, None]
    ).astype(jnp.int32)
    slot_rank = jnp.sum((jnp.cumsum(onehot, axis=0) - onehot) * onehot, axis=1)
    slot_ids = jnp.where(is_live, owner_ids * capacity + slot_rank, total_slots)
    send_values = (
        jnp.zeros((total_slots, channels), jnp.float32).at[slot_ids].set(innovations, mode="drop")
    )
    send_cells = jnp.zeros((total_slots,), jnp.int32).at[slot_ids].set(obs_cell, mode="drop")
    send_marks = jnp.zeros((total_slots,), jnp.float32).at[slot_ids].set(1.0, mode="drop")
    got_values, got_cells, got_marks = (
        lax.all_to_all(
            send_values.reshape(blocks, capacity, channels),
            "col",
            split_axis=0,
            concat_axis=0,
            tiled=True,
        ),
        lax.all_to_all(
            send_cells.reshape(blocks, capacity), "col", split_axis=0, concat_axis=0, tiled=True
        ),
        lax.all_to_all(
            send_marks.reshape(blocks, capacity), "col", split_axis=0, concat_axis=0, tiled=True
        ),
    )
    got_values = got_values.reshape(total_slots, channels)
    got_cells = got_cells.reshape(total_slots)
    got_marks = got_marks.reshape(total_slots)
    obs_index = got_cells
    obs_gain = got_marks[:, None] * obs_weights[None, :]

    def spread_back(weighted):
        back = jnp.dot(weighted, obs_jacobian.T, precision=lax.Precision.HIGHEST)
        grid = jnp.zeros((rows_here * columns, features), jnp.float32).at[obs_index].add(back)
        return grid.reshape(rows_here, columns, features)

    def adjoint_map(gradient):
        own_gradient = lax.dynamic_slice_in_dim(gradient, offset, quarter, 1)
        rounded = gradient.astype(jnp.bfloat16)
        static = jnp.dot(
            own_gradient.reshape(rows_here * quarter, features),
            static_root.T,
            precision=lax.Precision.HIGHEST,
        ).reshape(rows_here, quarter, features)
        projected = jnp.einsum(
            "kyxf,yxf->kyx", perturbations, rounded, preferred_element_type=jnp.float32
        )
        return (static, sweeps(projected, coeffs))

    residual = adjoint_map(spread_back(obs_gain * got_values))
    direction = residual
    state = (jnp.zeros_like(residual[0]), jnp.zeros_like(residual[1]))
    increment = jnp.zeros((rows_here, quarter, features), jnp.float32)
    norm_now = lax.psum(local_inner(residual, residual), ("mem", "col"))
    for iteration in range(ITERS):
        smoothed = sweeps(direction[1], coeffs).astype(jnp.bfloat16)
        partial_sum = jnp.einsum(
            "kyxf,kyx->yxf", perturbations, smoothed, preferred_element_type=jnp.float32
        )
        forward_static = jnp.dot(
            direction[0].reshape(rows_here * quarter, features),
            static_root,
            precision=lax.Precision.HIGHEST,
        ).reshape(rows_here, quarter, features)
        own_slice = lax.dynamic_slice_in_dim(partial_sum, offset, quarter, 1) + forward_static
        partial_sum = lax.dynamic_update_slice_in_dim(partial_sum, own_slice, offset, 1)
        image_part = lax.psum(partial_sum, "mem")
        own_image = lax.dynamic_slice_in_dim(image_part, offset, quarter, 1)
        image_part, own_image = (image_part, own_image)
        gathered = image_part.reshape(rows_here * columns, features)[obs_index]
        model_obs = jnp.dot(gathered, obs_jacobian, precision=lax.Precision.HIGHEST)
        adj_static, adj_ensemble = adjoint_map(spread_back(obs_gain * model_obs))
        image = (direction[0] + adj_static, direction[1] + adj_ensemble)
        step = norm_now / lax.psum(local_inner(direction, image), ("mem", "col"))
        residual = (residual[0] - step * image[0], residual[1] - step * image[1])
        norm_next = lax.psum(local_inner(residual, residual), ("mem", "col"))
        state = (state[0] + step * direction[0], state[1] + step * direction[1])
        increment = increment + step * own_image
        ratio = norm_next / norm_now
        direction = (residual[0] + ratio * direction[0], residual[1] + ratio * direction[1])
        norm_now = norm_next
    return (increment, state[0], state[1])


def solution(mesh):
    placed = (
        P("mem", "col", None, None),
        P(),
        P(),
        P("col", None),
        P(),
        P("col", None),
        P("col", None),
        P("col"),
        P("col"),
    )
    return jax.shard_map(
        shards,
        mesh=mesh,
        in_specs=placed,
        out_specs=(P("col", "mem", None), P("col", "mem", None), P("mem", "col", None)),
        check_vma=False,
    )
```

profile of v0, /device:TPU:0, one launch (start us, length us, event | category | flops | bytes accessed | tf_op | source)
XLA Modules:
  0.0 461.8 jit_solution(2602918814722738291)
XLA Ops:
  13.2 6.3 %all-to-all-start = ((s32[8,1,64]{2,1,0:T(1,128)}), s32[8,1,64]{2,1,0:T(1,128)S(1)}, u32[]{:S(2)}, u32[]{:S(2)}) async-start(s32[8,1,64]{2,1,0:T(1,128)} %all_to_all.15), calls=%async_computation | async-start | bytes 8192 | tf_op jit(solution)/shard_map/all_to_all | solution.py:93
  21.6 3.4 all-to-all-done
  25.0 3.3 all-to-all-start.1
  28.3 2.2 scatter_custom_fusion.2
  30.5 3.2 all-to-all-done.1
  33.7 3.4 all-to-all-start.2
  38.0 2.2 collective-permute-start
  41.5 2.9 collective-permute-done.2
  49.0 2.8 scatter_custom_fusion.3
  53.8 5.4 %collective-permute-start.1 = (f32[8,1,256]{2,1,0:T(1,128)S(1)}, f32[8,1,256]{2,1,0:T(1,128)S(1)}, u32[]{:S(2)}, u32[]{:S(2)}) collective-permute-start(f32[8,1,256]{2,1,0:T(1,128)S(1)} %get-tuple-element.46), channel_id=1, source_target_pairs={{0,1},{1,2},{2,3},{3,4},{4,5},{5,6},{6,7},{8,9},{9,10},{10,11},{11... | collective-permute-start | bytes 24584 | tf_op jit(solution)/shard_map/ppermute | solution.py:15
  62.5 3.8 collective-permute-start.4
  67.7 1.8 collective-permute-done.5
  69.7 3.8 collective-permute-start.6
  74.9 1.8 collective-permute-done.7
  76.9 3.8 collective-permute-start.8
  82.1 1.8 collective-permute-done.9
  84.1 3.8 collective-permute-start.10
  91.3 3.8 collective-permute-start.12
  98.5 3.8 collective-permute-start.14
  105.7 3.8 collective-permute-start.16
  116.0 46.8 %all-reduce.25.cloned.1.call-done = f32[4,256,128]{2,1,0:T(8,128)} async-done(((f32[4,256,128]{2,1,0:T(8,128)}), f32[4,256,128]{2,1,0:T(8,128)}) %all-reduce.25.cloned.1.call-update) | async-done | bytes 524304 | tf_op jit(solution)/shard_map/psum | solution.py:141
  162.7 2.1 gather_fusion
  165.6 2.8 scatter_custom_fusion.4
  168.5 2.4 fusion.6
  172.1 2.6 collective-permute-start.18
  175.9 2.7 collective-permute-done.19
  179.0 4.3 collective-permute-start.20
  186.6 3.8 collective-permute-start.22
  193.8 3.9 collective-permute-start.24
  204.2 41.1 %all-reduce.21 = (f32[]{:T(128)}, f32[]{:T(128)}) all-reduce(f32[]{:T(128)S(6)} %add.401, f32[]{:T(128)S(6)} %add.437), channel_id=1, replica_groups=mesh['mem'=4,'col'=8] {'mem','col'}, use_global_device_ids=true, to_apply=%region_9.10 | all-reduce | flops 2 | bytes 16 | tf_op jit(solution)/shard_map/psum | solution.py:128
  249.1 40.1 %psum.45 = f32[]{:T(128)} all-reduce(f32[]{:T(128)S(6)} %add.438), channel_id=1, replica_groups=mesh['mem'=4,'col'=8] {'mem','col'}, use_global_device_ids=true, to_apply=%region_17.18 | all-reduce | flops 1 | bytes 8 | tf_op jit(solution)/shard_map/psum | solution.py:150
  293.2 2.7 collective-permute-done.27
  296.2 4.3 collective-permute-start.28
  303.8 3.8 collective-permute-start.30
  311.0 3.8 collective-permute-start.32
  319.3 2.8 fusion.4
  323.2 47.0 %all-reduce.27.cloned.1.call-done = f32[4,256,128]{2,1,0:T(8,128)} async-done(((f32[4,256,128]{2,1,0:T(8,128)}), f32[4,256,128]{2,1,0:T(8,128)}) %all-reduce.27.cloned.1.call-update) | async-done | bytes 524304 | tf_op jit(solution)/shard_map/psum | solution.py:141
  370.2 2.1 gather_fusion.1
  373.0 2.8 scatter_custom_fusion.5
  375.9 2.4 fusion.2
  379.5 2.6 collective-permute-start.34
  383.4 2.7 collective-permute-done.35
  386.4 4.3 collective-permute-start.36
  392.0 1.8 collective-permute-done.37
  394.0 3.8 collective-permute-start.38
  399.2 1.8 collective-permute-done.39
  401.2 3.9 collective-permute-start.40
  410.3 41.0 %psum.47 = f32[]{:T(128)} all-reduce(f32[]{:T(128)S(6)} %add.476), channel_id=1, replica_groups=mesh['mem'=4,'col'=8] {'mem','col'}, use_global_device_ids=true, to_apply=%region_22.23 | all-reduce | flops 1 | bytes 8 | tf_op jit(solution)/shard_map/psum | solution.py:148
  (188 shorter events, 83.0 us)
Async XLA Ops:
  13.2 11.8 %all-to-all-start = ((s32[8,1,64]{2,1,0:T(1,128)}), s32[8,1,64]{2,1,0:T(1,128)S(1)}, u32[]{:S(2)}, u32[]{:S(2)}) async-start(s32[8,1,64]{2,1,0:T(1,128)} %all_to_all.15), calls=%async_computation | async-start | bytes 8192 | tf_op jit(solution)/shard_map/all_to_all | solution.py:93
  25.0 8.7 %all-to-all-start.1 = ((f32[8,1,64]{2,1,0:T(1,128)}), f32[8,1,64]{2,1,0:T(1,128)S(1)}, u32[]{:S(2)}, u32[]{:S(2)}) async-start(f32[8,1,64]{2,1,0:T(1,128)} %all_to_all.17), calls=%async_computation.1 | async-start | bytes 8192 | tf_op jit(solution)/shard_map/all_to_all | solution.py:96
  33.7 14.0 %all-to-all-start.2 = ((f32[8,64,128]{2,1,0:T(8,128)}), f32[8,64,128]{2,1,0:T(8,128)S(1)}, u32[]{:S(2)}, u32[]{:S(2)}) async-start(f32[8,64,128]{2,1,0:T(8,128)} %bitcast.8), calls=%async_computation.2 | async-start | bytes 524288 | tf_op jit(solution)/shard_map/all_to_all | solution.py:86
  37.2 125.6 %all-reduce.25.cloned.1.call-start = ((), (), s32[]{:S(2)}) async-start(), calls=%async_computation.3 | async-start | bytes 1048576 | tf_op jit(solution)/shard_map/psum | solution.py:141
  38.0 3.6 collective-permute-start
  40.2 4.2 collective-permute-start.2
  53.5 50.2 %copy-start.1 = (f32[128,128]{1,0:T(8,128)S(1)}, f32[128,128]{1,0:T(8,128)}, u32[]{:S(2)}) copy-start(f32[128,128]{1,0:T(8,128)} %param.10) | copy-start | bytes 196612
  53.8 6.8 %collective-permute-start.1 = (f32[8,1,256]{2,1,0:T(1,128)S(1)}, f32[8,1,256]{2,1,0:T(1,128)S(1)}, u32[]{:S(2)}, u32[]{:S(2)}) collective-permute-start(f32[8,1,256]{2,1,0:T(1,128)S(1)} %get-tuple-element.46), channel_id=1, source_target_pairs={{0,1},{1,2},{2,3},{3,4},{4,5},{5,6},{6,7},{8,9},{9,10},{10,11},{11... | collective-permute-start | bytes 24584 | tf_op jit(solution)/shard_map/ppermute | solution.py:15
  59.2 3.1 collective-permute-start.3
  62.5 5.1 %collective-permute-start.4 = (f32[8,1,256]{2,1,0:T(1,128)S(1)}, f32[8,1,256]{2,1,0:T(1,128)S(1)}, u32[]{:S(2)}, u32[]{:S(2)}) collective-permute-start(f32[8,1,256]{2,1,0:T(1,128)S(1)} %get-tuple-element.44), channel_id=1, source_target_pairs={{0,1},{1,2},{2,3},{3,4},{4,5},{5,6},{6,7},{8,9},{9,10},{10,11},{11... | collective-permute-start | bytes 24584 | tf_op jit(solution)/shard_map/ppermute | solution.py:15
  66.4 3.1 collective-permute-start.5
  69.7 5.2 %collective-permute-start.6 = (f32[8,1,256]{2,1,0:T(1,128)S(1)}, f32[8,1,256]{2,1,0:T(1,128)S(1)}, u32[]{:S(2)}, u32[]{:S(2)}) collective-permute-start(f32[8,1,256]{2,1,0:T(1,128)S(1)} %get-tuple-element.42), channel_id=1, source_target_pairs={{0,1},{1,2},{2,3},{3,4},{4,5},{5,6},{6,7},{8,9},{9,10},{10,11},{11... | collective-permute-start | bytes 24584 | tf_op jit(solution)/shard_map/ppermute | solution.py:15
  73.6 3.1 collective-permute-start.7
  76.9 5.2 %collective-permute-start.8 = (f32[8,1,256]{2,1,0:T(1,128)S(1)}, f32[8,1,256]{2,1,0:T(1,128)S(1)}, u32[]{:S(2)}, u32[]{:S(2)}) collective-permute-start(f32[8,1,256]{2,1,0:T(1,128)S(1)} %get-tuple-element.40), channel_id=1, source_target_pairs={{0,1},{1,2},{2,3},{3,4},{4,5},{5,6},{6,7},{8,9},{9,10},{10,11},{11... | collective-permute-start | bytes 24584 | tf_op jit(solution)/shard_map/ppermute | solution.py:15
  80.8 3.1 collective-permute-start.9
  84.1 5.2 %collective-permute-start.10 = (f32[8,1,256]{2,1,0:T(1,128)S(1)}, f32[8,1,256]{2,1,0:T(1,128)S(1)}, u32[]{:S(2)}, u32[]{:S(2)}) collective-permute-start(f32[8,1,256]{2,1,0:T(1,128)S(1)} %get-tuple-element.38), channel_id=1, source_target_pairs={{0,1},{1,2},{2,3},{3,4},{4,5},{5,6},{6,7},{8,9},{9,10},{10,11},{11... | collective-permute-start | bytes 24584 | tf_op jit(solution)/shard_map/ppermute | solution.py:15
  88.0 3.1 collective-permute-start.11
  91.3 5.2 %collective-permute-start.12 = (f32[8,1,256]{2,1,0:T(1,128)S(1)}, f32[8,1,256]{2,1,0:T(1,128)S(1)}, u32[]{:S(2)}, u32[]{:S(2)}) collective-permute-start(f32[8,1,256]{2,1,0:T(1,128)S(1)} %get-tuple-element.36), channel_id=1, source_target_pairs={{0,1},{1,2},{2,3},{3,4},{4,5},{5,6},{6,7},{8,9},{9,10},{10,11},{11... | collective-permute-start | bytes 24584 | tf_op jit(solution)/shard_map/ppermute | solution.py:15
  95.2 3.1 collective-permute-start.13
  98.5 6.1 %collective-permute-start.14 = (f32[8,1,256]{2,1,0:T(1,128)S(1)}, f32[8,1,256]{2,1,0:T(1,128)S(1)}, u32[]{:S(2)}, u32[]{:S(2)}) collective-permute-start(f32[8,1,256]{2,1,0:T(1,128)S(1)} %get-tuple-element.34), channel_id=1, source_target_pairs={{0,1},{1,2},{2,3},{3,4},{4,5},{5,6},{6,7},{8,9},{9,10},{10,11},{11... | collective-permute-start | bytes 24584 | tf_op jit(solution)/shard_map/ppermute | solution.py:15
  102.3 3.1 collective-permute-start.15
  105.7 6.3 %collective-permute-start.16 = (f32[8,1,256]{2,1,0:T(1,128)S(1)}, f32[8,1,256]{2,1,0:T(1,128)S(1)}, u32[]{:S(2)}, u32[]{:S(2)}) collective-permute-start(f32[8,1,256]{2,1,0:T(1,128)S(1)} %get-tuple-element.32), channel_id=1, source_target_pairs={{0,1},{1,2},{2,3},{3,4},{4,5},{5,6},{6,7},{8,9},{9,10},{10,11},{11... | collective-permute-start | bytes 24584 | tf_op jit(solution)/shard_map/ppermute | solution.py:15
  109.5 3.1 collective-permute-start.17
  115.9 254.3 %all-reduce.27.cloned.1.call-start = ((), (), s32[]{:S(2)}) async-start(), calls=%async_computation.4 | async-start | bytes 1048576 | tf_op jit(solution)/shard_map/psum | solution.py:141
  172.1 3.9 collective-permute-start.18
  174.6 4.1 collective-permute-start.19
  179.0 5.6 %collective-permute-start.20 = (f32[8,1,256]{2,1,0:T(1,128)S(1)}, f32[8,1,256]{2,1,0:T(1,128)S(1)}, u32[]{:S(2)}, u32[]{:S(2)}) collective-permute-start(f32[8,1,256]{2,1,0:T(1,128)S(1)} %get-tuple-element.28), channel_id=1, source_target_pairs={{0,1},{1,2},{2,3},{3,4},{4,5},{5,6},{6,7},{8,9},{9,10},{10,11},{11... | collective-permute-start | bytes 24584 | tf_op jit(solution)/shard_map/ppermute | solution.py:15
  183.3 3.1 collective-permute-start.21
  186.6 5.2 %collective-permute-start.22 = (f32[8,1,256]{2,1,0:T(1,128)S(1)}, f32[8,1,256]{2,1,0:T(1,128)S(1)}, u32[]{:S(2)}, u32[]{:S(2)}) collective-permute-start(f32[8,1,256]{2,1,0:T(1,128)S(1)} %get-tuple-element.26), channel_id=1, source_target_pairs={{0,1},{1,2},{2,3},{3,4},{4,5},{5,6},{6,7},{8,9},{9,10},{10,11},{11... | collective-permute-start | bytes 24584 | tf_op jit(solution)/shard_map/ppermute | solution.py:15
  190.5 3.1 collective-permute-start.23
  193.8 6.0 %collective-permute-start.24 = (f32[8,1,256]{2,1,0:T(1,128)S(1)}, f32[8,1,256]{2,1,0:T(1,128)S(1)}, u32[]{:S(2)}, u32[]{:S(2)}) collective-permute-start(f32[8,1,256]{2,1,0:T(1,128)S(1)} %get-tuple-element.24), channel_id=1, source_target_pairs={{0,1},{1,2},{2,3},{3,4},{4,5},{5,6},{6,7},{8,9},{9,10},{10,11},{11... | collective-permute-start | bytes 24584 | tf_op jit(solution)/shard_map/ppermute | solution.py:15
  197.7 3.1 collective-permute-start.25
  290.6 2.6 collective-permute-start.26
  291.9 4.0 collective-permute-start.27
  296.2 5.6 %collective-permute-start.28 = (f32[8,1,256]{2,1,0:T(1,128)S(1)}, f32[8,1,256]{2,1,0:T(1,128)S(1)}, u32[]{:S(2)}, u32[]{:S(2)}) collective-permute-start(f32[8,1,256]{2,1,0:T(1,128)S(1)} %get-tuple-element.20), channel_id=1, source_target_pairs={{0,1},{1,2},{2,3},{3,4},{4,5},{5,6},{6,7},{8,9},{9,10},{10,11},{11... | collective-permute-start | bytes 24584 | tf_op jit(solution)/shard_map/ppermute | solution.py:15
  300.5 3.1 collective-permute-start.29
  303.8 5.2 %collective-permute-start.30 = (f32[8,1,256]{2,1,0:T(1,128)S(1)}, f32[8,1,256]{2,1,0:T(1,128)S(1)}, u32[]{:S(2)}, u32[]{:S(2)}) collective-permute-start(f32[8,1,256]{2,1,0:T(1,128)S(1)} %get-tuple-element.18), channel_id=1, source_target_pairs={{0,1},{1,2},{2,3},{3,4},{4,5},{5,6},{6,7},{8,9},{9,10},{10,11},{11... | collective-permute-start | bytes 24584 | tf_op jit(solution)/shard_map/ppermute | solution.py:15
  307.7 3.1 collective-permute-start.31
  311.0 5.4 %collective-permute-start.32 = (f32[8,1,256]{2,1,0:T(1,128)S(1)}, f32[8,1,256]{2,1,0:T(1,128)S(1)}, u32[]{:S(2)}, u32[]{:S(2)}) collective-permute-start(f32[8,1,256]{2,1,0:T(1,128)S(1)} %get-tuple-element.16), channel_id=1, source_target_pairs={{0,1},{1,2},{2,3},{3,4},{4,5},{5,6},{6,7},{8,9},{9,10},{10,11},{11... | collective-permute-start | bytes 24584 | tf_op jit(solution)/shard_map/ppermute | solution.py:15
  314.9 3.1 collective-permute-start.33
  379.5 3.9 collective-permute-start.34
  382.0 4.0 collective-permute-start.35
  386.4 5.6 %collective-permute-start.36 = (f32[8,1,256]{2,1,0:T(1,128)S(1)}, f32[8,1,256]{2,1,0:T(1,128)S(1)}, u32[]{:S(2)}, u32[]{:S(2)}) collective-permute-start(f32[8,1,256]{2,1,0:T(1,128)S(1)} %get-tuple-element.12), channel_id=1, source_target_pairs={{0,1},{1,2},{2,3},{3,4},{4,5},{5,6},{6,7},{8,9},{9,10},{10,11},{11... | collective-permute-start | bytes 24584 | tf_op jit(solution)/shard_map/ppermute | solution.py:15
  390.7 3.1 collective-permute-start.37
  394.0 5.2 %collective-permute-start.38 = (f32[8,1,256]{2,1,0:T(1,128)S(1)}, f32[8,1,256]{2,1,0:T(1,128)S(1)}, u32[]{:S(2)}, u32[]{:S(2)}) collective-permute-start(f32[8,1,256]{2,1,0:T(1,128)S(1)} %get-tuple-element.10), channel_id=1, source_target_pairs={{0,1},{1,2},{2,3},{3,4},{4,5},{5,6},{6,7},{8,9},{9,10},{10,11},{11... | collective-permute-start | bytes 24584 | tf_op jit(solution)/shard_map/ppermute | solution.py:15
  397.9 3.1 collective-permute-start.39
  401.2 6.1 %collective-permute-start.40 = (f32[8,1,256]{2,1,0:T(1,128)S(1)}, f32[8,1,256]{2,1,0:T(1,128)S(1)}, u32[]{:S(2)}, u32[]{:S(2)}) collective-permute-start(f32[8,1,256]{2,1,0:T(1,128)S(1)} %get-tuple-element.8), channel_id=1, source_target_pairs={{0,1},{1,2},{2,3},{3,4},{4,5},{5,6},{6,7},{8,9},{9,10},{10,11},{11... | collective-permute-start | bytes 24584 | tf_op jit(solution)/shard_map/ppermute | solution.py:15
  405.1 3.1 collective-permute-start.41
  (7 other events, 156.4 us)
Sparse Core Ops, SparseCore 0:
  116.0 46.6 all-reduce.24
  323.3 46.8 all-reduce.26
where the time goes:
time: 464 us; the launch traced here: 462 us
  waiting for transfers between devices  137 us (30%)
  blocking collectives  122 us (26%)
  starting transfers between devices  118 us (25%)
  between operations  25.3 us (5%)
  other arithmetic  23.1 us (5%)
  local copies, waits for them, and re-layouts  18.8 us (4%)
  matrix products  17.4 us (4%)
    psum x2, waiting for transfers between devices, shards(): image_part = lax.psum(partial_sum, 'mem')  93.8 us
    ppermute x21, starting transfers between devices, extended(): lax.ppermute(lax.slice_in_dim(block, block.shape[dim] - width, None, axis...  77 us
    psum x1, blocking collectives, shards(): norm_now = lax.psum(local_inner(residual, residual), ('mem', 'col'))  41.1 us
    psum x1, blocking collectives, shards(): step = norm_now / lax.psum(local_inner(direction, image), ('mem', 'col'))  41 us
    psum x1, blocking collectives, shards(): norm_next = lax.psum(local_inner(residual, residual), ('mem', 'col'))  40.1 us
    ppermute x21, waiting for transfers between devices, extended(): lax.ppermute(lax.slice_in_dim(block, 0, width, axis=dim), axis, backward)  36.8 us
    ppermute x21, starting transfers between devices, extended(): lax.ppermute(lax.slice_in_dim(block, 0, width, axis=dim), axis, backward)  27.5 us
  transfers between devices with their start and end apart: 47, of which 25 were waited for; matrix products, arithmetic and copies ran while one was open for 2% of the time, Pallas kernels for 0%

commit v1 on v0

v1 whole, which is shorter than its diff:
```python
import functools

import jax
import jax.numpy as jnp
from jax import lax
from jax.experimental import pallas as pl
from jax.experimental.pallas import tpu as pltpu
from jax.sharding import PartitionSpec as P

NSWEEP = 4
F32 = jnp.float32
BF16 = jnp.bfloat16
MESH = pl.DeviceIdType.MESH
HIGH = lax.Precision.HIGHEST
OFFSETS = (-2, -1, 1, 2)
NT = (((1,), (1,)), ((), ()))


def loop(count, body):
    if count <= 16:
        for i in range(count):
            body(i)
    else:
        lax.fori_loop(0, count, lambda i, c: (body(i), c)[1], 0)


def iota(shape, dim):
    return lax.broadcasted_iota(jnp.int32, shape, dim)


def exact(a, b):
    return jnp.dot(a, b, precision=HIGH, preferred_element_type=F32)


def exact_t(a, b):
    return lax.dot_general(a, b, NT, precision=HIGH, preferred_element_type=F32)


def kernel(
    nm, nb, cap,
    pert_hbm, root_ref, jac_ref, innov_ref, weight_ref, scale_ref, owner_ref, cell_ref, count_ref,
    inc_ref, stat_ref, ens_ref,
    pert, outbox, inbox, scales, vert, left, right, centre, pbuf, gfull, fpart, fsend, frecv,
    sums_col, sums_mem, ens_b, ens_h, acc, wdiag,
    pert_sem, obs_send, obs_recv, ls_send, ls_recv, g_send, g_recv, p_send, p_recv,
    f_send, f_recv, sc_send, sc_recv, sm_send, sm_recv,
):
    mem = lax.axis_index("mem")
    col = lax.axis_index("col")
    members, rows, columns, feat = pert.shape
    obs_dev = innov_ref.shape[0]
    quarter = columns // nm
    own_cols = rows * quarter
    total_rows = 5 * rows
    half = 128
    nblk = columns // half

    load = pltpu.make_async_copy(pert_hbm, pert, pert_sem)
    load.start()

    for phase in range(2):
        for r in range(2 * rows):
            pbuf[phase, r] = jnp.zeros((members, columns), F32)
            pbuf[phase, 3 * rows + r] = jnp.zeros((members, columns), F32)
    scales[...] = jnp.zeros_like(scales)
    scales[2, 0:rows, :] = scale_ref[...]

    barrier = pltpu.get_barrier_semaphore()

    def greet_col(i):
        pl.semaphore_signal(
            barrier, inc=1, device_id={"col": lax.rem(col + i + 1, nb)}, device_id_type=MESH
        )

    loop(nb - 1, greet_col)
    for i in range(1, nm):
        pl.semaphore_signal(
            barrier, inc=1, device_id={"mem": lax.rem(mem + i, nm)}, device_id_type=MESH
        )

    owner = owner_ref[...]
    cell = cell_ref[...]
    lane = iota((1, obs_dev), 1)
    live = lane < count_ref[...]
    owner = jnp.where(live, owner, -1)
    held = (owner == iota((nb, obs_dev), 0)).astype(F32)
    before = (iota((obs_dev, obs_dev), 0) < iota((obs_dev, obs_dev), 1)).astype(F32).astype(BF16)
    earlier = jnp.dot(held.astype(BF16), before, preferred_element_type=F32)
    rank = jnp.sum(earlier * held, axis=0, keepdims=True)
    col_shift = columns.bit_length() - 1
    q_shift = quarter.bit_length() - 1
    grid_row = lax.shift_right_logical(cell, col_shift)
    part = lax.shift_right_logical(cell, q_shift) & (nm - 1)
    inner = cell & (quarter - 1)
    kind = iota((16, obs_dev), 0)
    facts = jnp.where(
        kind == 0, grid_row,
        jnp.where(kind == 1, part, jnp.where(kind == 2, inner, jnp.where(kind == 3, 1, 0))),
    ).astype(F32).astype(BF16)
    innov = innov_ref[...].astype(BF16)
    slot_id = iota((128, obs_dev), 0).astype(F32)

    def message(target, box, at):
        mine = jnp.where(owner == target, rank, -1.0)
        pick = (slot_id == mine).astype(F32).astype(BF16)
        box[at, 0:cap, :] = jnp.dot(
            pick[0:cap], innov, preferred_element_type=F32
        ).astype(BF16)
        box[at, cap:cap + 16, :] = lax.dot_general(
            facts, pick, NT, preferred_element_type=F32
        ).astype(BF16)

    def obs_copy(i):
        return pltpu.make_async_remote_copy(
            src_ref=outbox.at[i], dst_ref=inbox.at[i],
            send_sem=obs_send.at[i], recv_sem=obs_recv.at[i],
            device_id={"col": lax.rem(col + i, nb)}, device_id_type=MESH,
        )

    pl.semaphore_wait(barrier, nb - 1 + nm - 1)

    def halo_copy(buf_src, buf_dst, send, recv, o):
        return pltpu.make_async_remote_copy(
            src_ref=buf_src, dst_ref=buf_dst, send_sem=send.at[2 + o], recv_sem=recv.at[2 - o],
            device_id={"col": lax.rem(col + o + nb, nb)}, device_id_type=MESH,
        )

    def inside(o):
        return col + o < nb if o > 0 else col + o >= 0

    def ls_copy(o):
        return halo_copy(scales.at[2], scales.at[2 - o], ls_send, ls_recv, o)

    def each_halo(make, action):
        for o in OFFSETS:
            @pl.when(inside(o))
            def _(o=o):
                getattr(make(o), action)()

    def halo_wait(make_wait):
        for o in OFFSETS:
            @pl.when(inside(o))
            def _(o=o):
                make_wait(o)

    each_halo(ls_copy, "start")

    def send_obs(i):
        message(lax.rem(col + i + 1, nb), outbox, i + 1)
        obs_copy(i + 1).start()

    loop(nb - 1, send_obs)
    message(col, inbox, 0)

    def wait_ls(o):
        ls_copy(-o).wait_recv()

    halo_wait(wait_ls)

    first_lane = iota((members, columns), 1) == 0

    def scale_row(r):
        return jnp.broadcast_to(scales[r // rows, r % rows:r % rows + 1, :], (members, columns))

    for r in range(total_rows):
        here = scale_row(r)
        face = jnp.sqrt(here * pltpu.roll(here, 1, 1))
        face = jnp.where(first_lane, 0.0, face)
        left[r] = face
        right[r] = pltpu.roll(face, columns - 1, 1)
        if r < total_rows - 1:
            vert[r] = jnp.sqrt(here * scale_row(r + 1))
    for r in range(1, total_rows - 1):
        centre[r] = 1.0 - (vert[r - 1] + vert[r] + left[r] + right[r])

    def smooth(phase, keep):
        values = [pbuf[phase, r] for r in range(total_rows)]
        for s in range(2 * NSWEEP):
            new = list(values)
            for r in range(s + 1, total_rows - s - 1):
                a = values[r]
                new[r] = (
                    centre[r] * a + vert[r - 1] * values[r - 1] + vert[r] * values[r + 1]
                    + left[r] * pltpu.roll(a, 1, 1) + right[r] * pltpu.roll(a, columns - 1, 1)
                )
            values = new
            if s == NSWEEP - 1:
                for y in range(rows):
                    keep[y] = values[2 * rows + y]
        return [values[2 * rows + y] for y in range(rows)]

    diagonal = iota((half, half), 0) == iota((half, half), 1)

    def block(y, b):
        return pert[:, y, b * half:(b + 1) * half, :].reshape(members * half, feat)

    own_slice = pl.ds(pl.multiple_of(mem * quarter, quarter), quarter)

    def g_copy(phase, i):
        at = phase * nm + i
        return pltpu.make_async_remote_copy(
            src_ref=gfull.at[phase, :, own_slice, :], dst_ref=gfull.at[phase, :, own_slice, :],
            send_sem=g_send.at[at], recv_sem=g_recv.at[at],
            device_id={"mem": lax.rem(mem + i, nm)}, device_id_type=MESH,
        )

    def p_copy(phase, o):
        own = pbuf.at[phase, pl.ds(2 * rows, rows)]
        return pltpu.make_async_remote_copy(
            src_ref=own, dst_ref=pbuf.at[phase, pl.ds((2 - o) * rows, rows)],
            send_sem=p_send.at[phase * 5 + 2 + o], recv_sem=p_recv.at[phase * 5 + 2 - o],
            device_id={"col": lax.rem(col + o + nb, nb)}, device_id_type=MESH,
        )

    def f_copy(phase, i):
        at = phase * nm + i
        target = lax.rem(mem + i, nm)
        return pltpu.make_async_remote_copy(
            src_ref=fsend.at[
                phase, :, pl.ds(pl.multiple_of(target * quarter, quarter), quarter), :
            ],
            dst_ref=frecv.at[phase, i],
            send_sem=f_send.at[at], recv_sem=f_recv.at[at],
            device_id={"mem": target}, device_id_type=MESH,
        )

    def round_trip(phase, grad, keep):
        gfull[phase, :, own_slice, :] = grad.astype(BF16).reshape(rows, quarter, feat)
        for i in range(1, nm):
            g_copy(phase, i).start()
        static = exact_t(grad, root_ref[...])
        forward = exact(static, root_ref[...])
        if phase == 0:
            load.wait()
        for i in range(1, nm):
            g_copy(phase, i).wait_recv()
        for y in range(rows):
            for b in range(nblk):
                full = lax.dot_general(
                    block(y, b), gfull[phase, y, b * half:(b + 1) * half, :], NT,
                    preferred_element_type=F32,
                ).reshape(members, half, half)
                pbuf[phase, 2 * rows + y, :, b * half:(b + 1) * half] = jnp.sum(
                    jnp.where(diagonal[None], full, 0.0), axis=1
                )
        each_halo(lambda o: p_copy(phase, o), "start")
        halo_wait(lambda o: p_copy(phase, -o).wait_recv())
        weights = smooth(phase, keep)
        for b in range(nblk):
            for y in range(rows):
                line = weights[y][:, b * half:(b + 1) * half]
                for k in range(members):
                    wdiag[:, k * half:(k + 1) * half] = jnp.where(
                        diagonal, line[k:k + 1, :], 0.0
                    ).astype(BF16)
                piece = jnp.dot(wdiag[...], block(y, b), preferred_element_type=F32)
                fpart[y, b * half:(b + 1) * half, :] = piece
                fsend[phase, y, b * half:(b + 1) * half, :] = piece.astype(BF16)
        for i in range(1, nm):
            f_copy(phase, i).start()
        image = fpart[:, own_slice, :].reshape(own_cols, feat) + forward
        for i in range(1, nm):
            f_copy(phase, i).wait_recv()
            image = image + frecv[phase, i].astype(F32).reshape(own_cols, feat)
        return static, image

    place = iota((own_cols, cap), 0).astype(F32)
    ones = jnp.ones((cap, feat), BF16)
    acc[...] = jnp.zeros_like(acc)

    def gather_obs(i):
        told = inbox[i, cap:cap + 16, :].astype(F32)
        ours = (told[3:4] > 0.5) & (told[1:2] == mem.astype(F32))
        spot = jnp.where(ours, told[0:1] * quarter + told[2:3], -1.0)
        chosen = (place == spot[:, 0:cap]).astype(F32).astype(BF16)
        acc[0] += jnp.dot(chosen, inbox[i, 0:cap, :], preferred_element_type=F32)
        acc[1] += jnp.dot(chosen, ones, preferred_element_type=F32)

    gather_obs(0)

    def receive_obs(i):
        obs_copy(i + 1).wait_recv()
        gather_obs(i + 1)

    loop(nb - 1, receive_obs)
    gain = acc[1] * weight_ref[...]
    grad = exact_t(acc[0] * weight_ref[...], jac_ref[...])
    static_b, image_b = round_trip(0, grad, ens_b)
    model_b = exact(image_b, jac_ref[...])
    weighted = gain * model_b
    static_h, image_h = round_trip(1, exact_t(weighted, jac_ref[...]), ens_h)
    model_h = exact(image_h, jac_ref[...])

    def lanes(x):
        return jnp.sum(x, axis=0, keepdims=True)

    def pair(first, second, s_first, s_second):
        total = lanes(s_first * s_second)
        e = lanes(jnp.sum(first[...] * second[...], axis=0))
        for b in range(nblk):
            total = total + e[:, b * half:(b + 1) * half]
        return total

    line = iota((8, 128), 0)
    tile = jnp.zeros((8, 128), F32)
    for at, term in enumerate((
        pair(ens_b, ens_b, static_b, static_b),
        pair(ens_b, ens_h, static_b, static_h),
        pair(ens_h, ens_h, static_h, static_h),
        lanes(weighted * model_b),
        lanes(weighted * model_h),
        lanes(gain * model_h * model_h),
    )):
        tile = jnp.where(line == at, term, tile)
    sums_col[0] = tile

    def sc_copy(i):
        return pltpu.make_async_remote_copy(
            src_ref=sums_col.at[0], dst_ref=sums_col.at[i],
            send_sem=sc_send.at[i], recv_sem=sc_recv.at[i],
            device_id={"col": lax.rem(col + i, nb)}, device_id_type=MESH,
        )

    def sm_copy(i):
        return pltpu.make_async_remote_copy(
            src_ref=sums_mem.at[0], dst_ref=sums_mem.at[i],
            send_sem=sm_send.at[i], recv_sem=sm_recv.at[i],
            device_id={"mem": lax.rem(mem + i, nm)}, device_id_type=MESH,
        )

    loop(nb - 1, lambda i: sc_copy(i + 1).start())
    loop(nb - 1, lambda i: sc_copy(i + 1).wait_recv())
    sums_mem[0] = jnp.sum(sums_col[...], axis=0)
    for i in range(1, nm):
        sm_copy(i).start()
    for i in range(1, nm):
        sm_copy(i).wait_recv()
    sums = jnp.sum(jnp.sum(sums_mem[...], axis=0), axis=1, keepdims=True)
    bb, bh, hh, zbb, zbh, zhh = (sums[i:i + 1] for i in range(6))

    step = bb / (bb + bh)
    rest = 1.0 - step
    norm = rest * rest * bb - 2.0 * step * rest * bh + step * step * hh
    along = rest + norm / bb
    curve = (
        along * along * (bb + zbb) - 2.0 * along * step * (bh + zbh) + step * step * (hh + zhh)
    )
    later = norm / curve
    first = step + later * along
    second = -later * step
    inc_ref[...] = (first * image_b + second * image_h).reshape(inc_ref.shape)
    stat_ref[...] = (first * static_b + second * static_h).reshape(stat_ref.shape)
    for y in range(rows):
        ens_ref[:, y, :] = first * ens_b[y] + second * ens_h[y]

    loop(nb - 1, lambda i: obs_copy(i + 1).wait_send())
    loop(nb - 1, lambda i: sc_copy(i + 1).wait_send())
    halo_wait(lambda o: ls_copy(o).wait_send())
    for phase in range(2):
        halo_wait(lambda o: p_copy(phase, o).wait_send())
        for i in range(1, nm):
            g_copy(phase, i).wait_send()
            f_copy(phase, i).wait_send()
    for i in range(1, nm):
        sm_copy(i).wait_send()


def shards(
    perturbations, static_root, obs_jacobian, innovations, obs_weights, length_scale,
    obs_owner, obs_cell, obs_count,
):
    members, rows, columns, feat = perturbations.shape
    nm, nb = lax.axis_size("mem"), lax.axis_size("col")
    obs_dev = innovations.shape[0]
    cap = max(16, 2 * obs_dev // nb)
    quarter = columns // nm
    own_cols = rows * quarter
    total_rows = 5 * rows
    vmem = pl.BlockSpec(memory_space=pltpu.VMEM)
    dma = pltpu.SemaphoreType.DMA
    strip = pltpu.VMEM((total_rows, members, columns), F32)
    return pl.pallas_call(
        functools.partial(kernel, nm, nb, cap),
        out_shape=(
            jax.ShapeDtypeStruct((rows, quarter, feat), F32),
            jax.ShapeDtypeStruct((rows, quarter, feat), F32),
            jax.ShapeDtypeStruct((members, rows, columns), F32),
        ),
        in_specs=[pl.BlockSpec(memory_space=pl.ANY)] + [vmem] * 8,
        out_specs=(vmem,) * 3,
        scratch_shapes=[
            pltpu.VMEM(perturbations.shape, BF16),
            pltpu.VMEM((nb, cap + 16, feat), BF16),
            pltpu.VMEM((nb, cap + 16, feat), BF16),
            pltpu.VMEM((5, 8, columns), F32),
            strip, strip, strip, strip,
            pltpu.VMEM((2, total_rows, members, columns), F32),
            pltpu.VMEM((2, rows, columns, feat), BF16),
            pltpu.VMEM((rows, columns, feat), F32),
            pltpu.VMEM((2, rows, columns, feat), BF16),
            pltpu.VMEM((2, nm, rows, quarter, feat), BF16),
            pltpu.VMEM((nb, 8, 128), F32),
            pltpu.VMEM((nm, 8, 128), F32),
            pltpu.VMEM((rows, members, columns), F32),
            pltpu.VMEM((rows, members, columns), F32),
            pltpu.VMEM((2, own_cols, feat), F32),
            pltpu.VMEM((128, members * 128), BF16),
            dma,
            dma((nb,)), dma((nb,)),
            dma((5,)), dma((5,)),
            dma((2 * nm,)), dma((2 * nm,)),
            dma((10,)), dma((10,)),
            dma((2 * nm,)), dma((2 * nm,)),
            dma((nb,)), dma((nb,)),
            dma((nm,)), dma((nm,)),
        ],
        compiler_params=pltpu.CompilerParams(
            collective_id=0, has_side_effects=True, vmem_limit_bytes=40 * 1024 * 1024
        ),
    )(
        perturbations, static_root, obs_jacobian, innovations, obs_weights.reshape(1, -1),
        length_scale, obs_owner.reshape(1, -1), obs_cell.reshape(1, -1), obs_count.reshape(1, 1),
    )


def solution(mesh):
    placed = (
        P("mem", "col", None, None),
        P(),
        P(),
        P("col", None),
        P(),
        P("col", None),
        P("col", None),
        P("col"),
        P("col"),
    )
    return jax.shard_map(
        shards,
        mesh=mesh,
        in_specs=placed,
        out_specs=(P("col", "mem", None), P("col", "mem", None), P("mem", "col", None)),
        check_vma=False,
    )
```

time: 464 us -> 60.8 us (0.13)
  waiting for transfers between devices: 137 us -> 0 us
  blocking collectives: 122 us -> 0 us
  starting transfers between devices: 118 us -> 0 us
  Pallas kernels: 0 us -> 50.3 us
  between operations: 25.3 us -> 1.3 us
  other arithmetic: 23.1 us -> 0 us
  matrix products: 17.4 us -> 0 us
  local copies, waits for them, and re-layouts: 18.8 us -> 8.79 us
    psum x3 -> x0, blocking collectives: 122 us -> none  [the longest x1 41.1 us: shards(): norm_now = lax.psum(local_inner(residual, residual), ('mem', 'col'))]
    ppermute x42 -> x0, starting transfers between devices: 105 us -> none  [the longest x21 77 us: extended(): lax.ppermute(lax.slice_in_dim(block, block.shape[dim] - width, None, axis...]
    psum x2 -> x0, waiting for transfers between devices: 93.8 us -> none  [shards(): image_part = lax.psum(partial_sum, 'mem')]
    pallas_call x0 -> x1, Pallas kernels: none -> 50.3 us  [shards(): pl.pallas_call(functools.partial(kernel, nm, nb, cap), out_shape=(jax.Sha...]
    ppermute x42 -> x0, waiting for transfers between devices: 36.9 us -> none  [the longest x21 36.8 us: extended(): lax.ppermute(lax.slice_in_dim(block, 0, width, axis=dim), axis, backward)]
    dot_general x15 -> x0, matrix products: 17.4 us -> none  [the longest x3 6.39 us: adjoint_map(): jnp.einsum('kyxf,yxf->kyx', perturbations, rounded, preferred_element_typ...]
    all_to_all x3 -> x0, starting transfers between devices: 13 us -> none  [the longest x1 6.33 us: shards(): lax.all_to_all(send_cells.reshape(blocks, capacity), 'col', split_axis=0,...]
    scatter-add x3 -> x0, other arithmetic: 8.44 us -> none  [spread_back(): jnp.zeros((rows_here * columns, features), jnp.float32).at[obs_index]]
  transfers between devices with their start and end apart: 47 -> 0, of which waited for: 25 -> 0; matrix products, arithmetic and copies ran while one was open for 2% -> 0% of each run, Pallas kernels for 0% -> 0%
where the time goes in v1:
time: 60.8 us; the launch traced here: 60.4 us
  Pallas kernels  50.3 us (83%)
  local copies, waits for them, and re-layouts  8.79 us (14%)
  between operations  1.3 us (2%)
    pallas_call x1, Pallas kernels, shards(): pl.pallas_call(functools.partial(kernel, nm, nb, cap), out_shape=(jax.Sha...  50.3 us
    unnamed x19, local copies, waits for them, and re-layouts  8.79 us

profile of v1, /device:TPU:0, one launch (start us, length us, event | category | flops | bytes accessed | tf_op | source)
XLA Modules:
  0.0 60.4 jit_solution(3974063187939257621)
XLA Ops:
  1.3 0.0 copy-start
  1.3 1.6 %copy-done = bf16[8,4,256,128]{3,2,1,0:T(8,128)(2,1)S(1)} copy-done((bf16[8,4,256,128]{3,2,1,0:T(8,128)(2,1)S(1)}, bf16[8,4,256,128]{3,2,1,0:T(8,128)(2,1)}, u32[]{:S(2)}) %copy-start) | copy-done | bytes 2097176
  2.9 0.0 copy-start.1
  2.9 0.9 %copy-done.1 = f32[256,128]{1,0:T(8,128)S(1)} copy-done((f32[256,128]{1,0:T(8,128)S(1)}, f32[256,128]{1,0:T(8,128)}, u32[]{:S(2)}) %copy-start.1) | copy-done | bytes 131096
  3.8 0.0 copy-start.2
  3.8 0.8 %copy-done.2 = f32[128,128]{1,0:T(8,128)S(1)} copy-done((f32[128,128]{1,0:T(8,128)S(1)}, f32[128,128]{1,0:T(8,128)}, u32[]{:S(2)}) %copy-start.2) | copy-done | bytes 65560
  4.6 0.0 copy-start.3
  4.6 0.8 %copy-done.3 = f32[128,128]{1,0:T(8,128)S(1)} copy-done((f32[128,128]{1,0:T(8,128)S(1)}, f32[128,128]{1,0:T(8,128)}, u32[]{:S(2)}) %copy-start.3) | copy-done | bytes 65560
  5.5 0.0 copy-start.4
  5.5 0.7 %copy-done.4 = f32[4,256]{1,0:T(4,128)S(1)} copy-done((f32[4,256]{1,0:T(4,128)S(1)}, f32[4,256]{1,0:T(4,128)}, u32[]{:S(2)}) %copy-start.4) | copy-done | bytes 4120
  6.1 0.0 copy-start.5
  6.1 0.7 %copy-done.5 = s32[256,1]{0,1:T(1,128)S(1)} copy-done((s32[256,1]{0,1:T(1,128)S(1)}, s32[256,1]{0,1:T(1,128)}, u32[]{:S(2)}) %copy-start.5) | copy-done | bytes 1048
  6.8 0.0 copy-start.6
  6.8 0.7 %copy-done.6 = s32[256]{0:T(256)S(1)} copy-done((s32[256]{0:T(256)S(1)}, s32[256]{0:T(256)}, u32[]{:S(2)}) %copy-start.6) | copy-done | bytes 1048
  7.5 0.0 copy-start.7
  7.5 0.7 %copy-done.7 = f32[128]{0:T(128)S(1)} copy-done((f32[128]{0:T(128)S(1)}, f32[128]{0:T(128)}, u32[]{:S(2)}) %copy-start.7) | copy-done | bytes 536
  8.2 50.3 %shard_map.112 = (f32[4,64,128]{2,1,0:T(8,128)S(1)}, f32[4,64,128]{2,1,0:T(8,128)S(1)}, f32[8,4,256]{2,1,0:T(4,128)S(1)}) custom-call(bf16[8,4,256,128]{3,2,1,0:T(8,128)(2,1)S(1)} %copy-done, f32[128,128]{1,0:T(8,128)S(1)} %copy-done.2, f32[128,128]{1,0:T(8,128)S(1)} %copy-done.3, f32[256,128]{1,0:T(8,128)S(1)} %copy-done.1, f32[1,128]{1,0:T(1,128)S(1)} %bitcast.7, ...), custom_call_target="tpu_custom_call" | custom-call | tf_op jit(solution)/shard_map/pallas_call | solution.py:382
  58.5 0.7 %copy.16 = f32[4,64,128]{2,1,0:T(8,128)} copy(f32[4,64,128]{2,1,0:T(8,128)S(1)} %get-tuple-element.6) | data formatting | bytes 262144
  59.1 0.7 %copy.17 = f32[4,64,128]{2,1,0:T(8,128)} copy(f32[4,64,128]{2,1,0:T(8,128)S(1)} %get-tuple-element.7) | data formatting | bytes 262144
  59.8 0.6 %copy.18 = f32[8,4,256]{2,1,0:T(4,128)} copy(f32[8,4,256]{2,1,0:T(4,128)S(1)} %get-tuple-element.8) | data formatting | bytes 65536
Async XLA Ops:
  1.3 1.6 %copy-start = (bf16[8,4,256,128]{3,2,1,0:T(8,128)(2,1)S(1)}, bf16[8,4,256,128]{3,2,1,0:T(8,128)(2,1)}, u32[]{:S(2)}) copy-start(bf16[8,4,256,128]{3,2,1,0:T(8,128)(2,1)} %pert_hbm.1) | copy-start | bytes 6291460
  2.9 0.9 %copy-start.1 = (f32[256,128]{1,0:T(8,128)S(1)}, f32[256,128]{1,0:T(8,128)}, u32[]{:S(2)}) copy-start(f32[256,128]{1,0:T(8,128)} %innov_ref.1) | copy-start | bytes 393220
  3.8 0.8 %copy-start.2 = (f32[128,128]{1,0:T(8,128)S(1)}, f32[128,128]{1,0:T(8,128)}, u32[]{:S(2)}) copy-start(f32[128,128]{1,0:T(8,128)} %root_ref.1) | copy-start | bytes 196612
  4.6 0.8 %copy-start.3 = (f32[128,128]{1,0:T(8,128)S(1)}, f32[128,128]{1,0:T(8,128)}, u32[]{:S(2)}) copy-start(f32[128,128]{1,0:T(8,128)} %jac_ref.1) | copy-start | bytes 196612
  5.5 0.7 %copy-start.4 = (f32[4,256]{1,0:T(4,128)S(1)}, f32[4,256]{1,0:T(4,128)}, u32[]{:S(2)}) copy-start(f32[4,256]{1,0:T(4,128)} %scale_ref.1) | copy-start | bytes 12292
  6.1 0.7 %copy-start.5 = (s32[256,1]{0,1:T(1,128)S(1)}, s32[256,1]{0,1:T(1,128)}, u32[]{:S(2)}) copy-start(s32[256,1]{0,1:T(1,128)} %param.15) | copy-start | bytes 3076
  6.8 0.7 %copy-start.6 = (s32[256]{0:T(256)S(1)}, s32[256]{0:T(256)}, u32[]{:S(2)}) copy-start(s32[256]{0:T(256)} %param.16) | copy-start | bytes 3076
  7.5 0.7 %copy-start.7 = (f32[128]{0:T(128)S(1)}, f32[128]{0:T(128)}, u32[]{:S(2)}) copy-start(f32[128]{0:T(128)} %param.13) | copy-start | bytes 1540

commit v2 on v1

--- a/solution.py
+++ b/solution.py
@@ -11,8 +11,8 @@
 F32 = jnp.float32
 BF16 = jnp.bfloat16
 MESH = pl.DeviceIdType.MESH
-HIGH = lax.Precision.HIGHEST
 OFFSETS = (-2, -1, 1, 2)
+NN = (((1,), (0,)), ((), ()))
 NT = (((1,), (1,)), ((), ()))
 
 
@@ -28,21 +28,37 @@
     return lax.broadcasted_iota(jnp.int32, shape, dim)
 
 
+def halves(a):
+    high = a.astype(BF16)
+    return high, (a - high.astype(F32)).astype(BF16)
+
+
+def product(a, b, dims):
+    a_high, a_low = halves(a)
+    b_high, b_low = halves(b)
+
+    def dot(x, y):
+        return lax.dot_general(x, y, dims, preferred_element_type=F32)
+
+    return dot(a_high, b_high) + (dot(a_high, b_low) + dot(a_low, b_high))
+
+
 def exact(a, b):
-    return jnp.dot(a, b, precision=HIGH, preferred_element_type=F32)
+    return product(a, b, NN)
 
 
 def exact_t(a, b):
-    return lax.dot_general(a, b, NT, precision=HIGH, preferred_element_type=F32)
+    return product(a, b, NT)
 
 
 def kernel(
     nm, nb, cap,
-    pert_hbm, root_ref, jac_ref, innov_ref, weight_ref, scale_ref, owner_ref, cell_ref, count_ref,
+    pert_hbm, root_hbm, jac_hbm, innov_hbm, weight_hbm, scale_hbm, owner_hbm, cell_hbm, count_hbm,
     inc_ref, stat_ref, ens_ref,
-    pert, outbox, inbox, scales, vert, left, right, centre, pbuf, gfull, fpart, fsend, frecv,
-    sums_col, sums_mem, ens_b, ens_h, acc, wdiag,
-    pert_sem, obs_send, obs_recv, ls_send, ls_recv, g_send, g_recv, p_send, p_recv,
+    pert, root_ref, jac_ref, innov_ref, weight_ref, scale_ref, owner_ref, cell_ref, count_ref,
+    outbox, inbox, scales, vert, left, right, centre, pbuf, gfull, fpart, fsend, frecv,
+    sums_col, sums_mem, ens_b, ens_h, grads, counts, wdiag,
+    load_sem, obs_send, obs_recv, ls_send, ls_recv, g_send, g_recv, p_send, p_recv,
     f_send, f_recv, sc_send, sc_recv, sm_send, sm_recv,
 ):
     mem = lax.axis_index("mem")
@@ -55,15 +71,22 @@
     half = 128
     nblk = columns // half
 
-    load = pltpu.make_async_copy(pert_hbm, pert, pert_sem)
-    load.start()
+    loads = [
+        pltpu.make_async_copy(source, target, load_sem.at[i])
+        for i, (source, target) in enumerate((
+            (owner_hbm, owner_ref), (cell_hbm, cell_ref), (count_hbm, count_ref),
+            (scale_hbm, scale_ref), (innov_hbm, innov_ref), (weight_hbm, weight_ref),
+            (jac_hbm, jac_ref), (root_hbm, root_ref), (pert_hbm, pert),
+        ))
+    ]
+    for load in loads:
+        load.start()
 
     for phase in range(2):
         for r in range(2 * rows):
             pbuf[phase, r] = jnp.zeros((members, columns), F32)
             pbuf[phase, 3 * rows + r] = jnp.zeros((members, columns), F32)
     scales[...] = jnp.zeros_like(scales)
-    scales[2, 0:rows, :] = scale_ref[...]
 
     barrier = pltpu.get_barrier_semaphore()
 
@@ -77,6 +100,10 @@
         pl.semaphore_signal(
             barrier, inc=1, device_id={"mem": lax.rem(mem + i, nm)}, device_id_type=MESH
         )
+
+    for load in loads[:-1]:
+        load.wait()
+    scales[2, 0:rows, :] = scale_ref[...]
 
     owner = owner_ref[...]
     cell = cell_ref[...]
@@ -97,7 +124,7 @@
         kind == 0, grid_row,
         jnp.where(kind == 1, part, jnp.where(kind == 2, inner, jnp.where(kind == 3, 1, 0))),
     ).astype(F32).astype(BF16)
-    innov = innov_ref[...].astype(BF16)
+    innov = jnp.concatenate(halves(innov_ref[...]), axis=1)
     slot_id = iota((128, obs_dev), 0).astype(F32)
 
     def message(target, box, at):
@@ -106,9 +133,10 @@
         box[at, 0:cap, :] = jnp.dot(
             pick[0:cap], innov, preferred_element_type=F32
         ).astype(BF16)
-        box[at, cap:cap + 16, :] = lax.dot_general(
+        box[at, cap:cap + 16, 0:128] = lax.dot_general(
             facts, pick, NT, preferred_element_type=F32
         ).astype(BF16)
+        box[at, cap:cap + 16, feat:2 * feat] = jnp.zeros((16, feat), BF16)
 
     def obs_copy(i):
         return pltpu.make_async_remote_copy(
@@ -225,15 +253,17 @@
         )
 
     def round_trip(phase, grad, keep):
-        gfull[phase, :, own_slice, :] = grad.astype(BF16).reshape(rows, quarter, feat)
-        for i in range(1, nm):
-            g_copy(phase, i).start()
+        if phase > 0:
+            gfull[phase, :, own_slice, :] = grad.astype(BF16).reshape(rows, quarter, feat)
+            for i in range(1, nm):
+                g_copy(phase, i).start()
         static = exact_t(grad, root_ref[...])
         forward = exact(static, root_ref[...])
         if phase == 0:
-            load.wait()
-        for i in range(1, nm):
-            g_copy(phase, i).wait_recv()
+            loads[-1].wait()
+        if phase > 0:
+            for i in range(1, nm):
+                g_copy(phase, i).wait_recv()
         for y in range(rows):
             for b in range(nblk):
                 full = lax.dot_general(
@@ -256,40 +286,42 @@
                 piece = jnp.dot(wdiag[...], block(y, b), preferred_element_type=F32)
                 fpart[y, b * half:(b + 1) * half, :] = piece
                 fsend[phase, y, b * half:(b + 1) * half, :] = piece.astype(BF16)
-        for i in range(1, nm):
-            f_copy(phase, i).start()
+            for i in range(1, nm):
+                @pl.when(lax.rem(mem + i, nm) * quarter // half == b)
+                def _(i=i):
+                    f_copy(phase, i).start()
         image = fpart[:, own_slice, :].reshape(own_cols, feat) + forward
         for i in range(1, nm):
             f_copy(phase, i).wait_recv()
             image = image + frecv[phase, i].astype(F32).reshape(own_cols, feat)
         return static, image
 
-    place = iota((own_cols, cap), 0).astype(F32)
-    ones = jnp.ones((cap, feat), BF16)
-    acc[...] = jnp.zeros_like(acc)
-
-    def gather_obs(i):
-        told = inbox[i, cap:cap + 16, :].astype(F32)
-        ours = (told[3:4] > 0.5) & (told[1:2] == mem.astype(F32))
-        spot = jnp.where(ours, told[0:1] * quarter + told[2:3], -1.0)
-        chosen = (place == spot[:, 0:cap]).astype(F32).astype(BF16)
-        acc[0] += jnp.dot(chosen, inbox[i, 0:cap, :], preferred_element_type=F32)
-        acc[1] += jnp.dot(chosen, ones, preferred_element_type=F32)
-
-    gather_obs(0)
-
-    def receive_obs(i):
-        obs_copy(i + 1).wait_recv()
-        gather_obs(i + 1)
-
-    loop(nb - 1, receive_obs)
-    gain = acc[1] * weight_ref[...]
-    grad = exact_t(acc[0] * weight_ref[...], jac_ref[...])
+    gain_map = exact_t(jac_ref[...] * weight_ref[...], jac_ref[...])
+    loop(nb - 1, lambda i: obs_copy(i + 1).wait_recv())
+    slots = nb * cap
+    told = jnp.concatenate(
+        [inbox[i, cap:cap + 16, 0:128].astype(F32)[:, 0:cap] for i in range(nb)], axis=1
+    )
+    spot = (told[0:1] * nm + told[1:2]) * quarter + told[2:3]
+    spot = jnp.where(told[3:4] > 0.5, spot, -1.0)
+    sent = jnp.concatenate(
+        [inbox[:, 0:cap, :].reshape(slots, 2 * feat), jnp.ones((slots, feat), BF16)], axis=1
+    )
+    place = iota((columns, slots), 0).astype(F32)
+    for y in range(rows):
+        chosen = (place == spot - y * columns).astype(F32).astype(BF16)
+        found = jnp.dot(chosen, sent, preferred_element_type=F32)
+        counts[y] = found[:, 2 * feat:]
+        total = (found[:, :feat] + found[:, feat:2 * feat]) * weight_ref[...]
+        row_grad = exact_t(total, jac_ref[...])
+        grads[y] = row_grad
+        gfull[0, y] = row_grad.astype(BF16)
+    grad = grads[:, own_slice, :].reshape(own_cols, feat)
+    count = counts[:, own_slice, :].reshape(own_cols, feat)
     static_b, image_b = round_trip(0, grad, ens_b)
-    model_b = exact(image_b, jac_ref[...])
-    weighted = gain * model_b
-    static_h, image_h = round_trip(1, exact_t(weighted, jac_ref[...]), ens_h)
-    model_h = exact(image_h, jac_ref[...])
+    back_b = count * exact(image_b, gain_map)
+    static_h, image_h = round_trip(1, back_b, ens_h)
+    back_h = count * exact(image_h, gain_map)
 
     def lanes(x):
         return jnp.sum(x, axis=0, keepdims=True)
@@ -307,9 +339,9 @@
         pair(ens_b, ens_b, static_b, static_b),
         pair(ens_b, ens_h, static_b, static_h),
         pair(ens_h, ens_h, static_h, static_h),
-        lanes(weighted * model_b),
-        lanes(weighted * model_h),
-        lanes(gain * model_h * model_h),
+        lanes(image_b * back_b),
+        lanes(image_h * back_b),
+        lanes(image_h * back_h),
     )):
         tile = jnp.where(line == at, term, tile)
     sums_col[0] = tile
@@ -359,7 +391,8 @@
     for phase in range(2):
         halo_wait(lambda o: p_copy(phase, o).wait_send())
         for i in range(1, nm):
-            g_copy(phase, i).wait_send()
+            if phase > 0:
+                g_copy(phase, i).wait_send()
             f_copy(phase, i).wait_send()
     for i in range(1, nm):
         sm_copy(i).wait_send()
@@ -374,7 +407,6 @@
     obs_dev = innovations.shape[0]
     cap = max(16, 2 * obs_dev // nb)
     quarter = columns // nm
-    own_cols = rows * quarter
     total_rows = 5 * rows
     vmem = pl.BlockSpec(memory_space=pltpu.VMEM)
     dma = pltpu.SemaphoreType.DMA
@@ -386,12 +418,20 @@
             jax.ShapeDtypeStruct((rows, quarter, feat), F32),
             jax.ShapeDtypeStruct((members, rows, columns), F32),
         ),
-        in_specs=[pl.BlockSpec(memory_space=pl.ANY)] + [vmem] * 8,
+        in_specs=[pl.BlockSpec(memory_space=pltpu.HBM)] * 9,
         out_specs=(vmem,) * 3,
         scratch_shapes=[
             pltpu.VMEM(perturbations.shape, BF16),
-            pltpu.VMEM((nb, cap + 16, feat), BF16),
-            pltpu.VMEM((nb, cap + 16, feat), BF16),
+            pltpu.VMEM(static_root.shape, F32),
+            pltpu.VMEM(obs_jacobian.shape, F32),
+            pltpu.VMEM(innovations.shape, F32),
+            pltpu.VMEM((1, feat), F32),
+            pltpu.VMEM(length_scale.shape, F32),
+            pltpu.VMEM((1, obs_dev), jnp.int32),
+            pltpu.VMEM((1, obs_dev), jnp.int32),
+            pltpu.VMEM((1, 1), jnp.int32),
+            pltpu.VMEM((nb, cap + 16, 2 * feat), BF16),
+            pltpu.VMEM((nb, cap + 16, 2 * feat), BF16),
             pltpu.VMEM((5, 8, columns), F32),
             strip, strip, strip, strip,
             pltpu.VMEM((2, total_rows, members, columns), F32),
@@ -403,9 +443,10 @@
             pltpu.VMEM((nm, 8, 128), F32),
             pltpu.VMEM((rows, members, columns), F32),
             pltpu.VMEM((rows, members, columns), F32),
-            pltpu.VMEM((2, own_cols, feat), F32),
+            pltpu.VMEM((rows, columns, feat), F32),
+            pltpu.VMEM((rows, columns, feat), F32),
             pltpu.VMEM((128, members * 128), BF16),
-            dma,
+            dma((9,)),
             dma((nb,)), dma((nb,)),
             dma((5,)), dma((5,)),
             dma((2 * nm,)), dma((2 * nm,)),
@@ -415,7 +456,7 @@
             dma((nm,)), dma((nm,)),
         ],
         compiler_params=pltpu.CompilerParams(
-            collective_id=0, has_side_effects=True, vmem_limit_bytes=40 * 1024 * 1024
+            collective_id=0, has_side_effects=True, vmem_limit_bytes=62 * 1024 * 1024
         ),
     )(
         perturbations, static_root, obs_jacobian, innovations, obs_weights.reshape(1, -1),

time: 60.8 us -> 55.4 us (0.911)
  local copies, waits for them, and re-layouts: 8.79 us -> 4.51 us
  Pallas kernels: 50.3 us -> 49.3 us
    unnamed x19 -> x3, local copies, waits for them, and re-layouts: 8.79 us -> 4.51 us
    pallas_call x1, Pallas kernels: 50.3 us -> 49.3 us  [shards(): pl.pallas_call(functools.partial(kernel, nm, nb, cap), out_shape=(jax.Sha...]
where the time goes in v2:
time: 55.4 us; the launch traced here: 55.1 us
  Pallas kernels  49.3 us (89%)
  local copies, waits for them, and re-layouts  4.51 us (8%)
  between operations  1.29 us (2%)
    pallas_call x1, Pallas kernels, shards(): pl.pallas_call(functools.partial(kernel, nm, nb, cap), out_shape=(jax.Sha...  49.3 us
    unnamed x3, local copies, waits for them, and re-layouts  4.51 us

profile of v2, /device:TPU:0, one launch (start us, length us, event | category | flops | bytes accessed | tf_op | source)
XLA Modules:
  0.0 55.1 jit_solution(1180469963035033359)
XLA Ops:
  1.3 49.3 %shard_map.112 = (f32[4,64,128]{2,1,0:T(8,128)}, f32[4,64,128]{2,1,0:T(8,128)}, f32[8,4,256]{2,1,0:T(4,128)}) custom-call(bf16[8,4,256,128]{3,2,1,0:T(8,128)(2,1)} %pert_hbm.1, f32[128,128]{1,0:T(8,128)} %root_hbm.1, f32[128,128]{1,0:T(8,128)} %jac_hbm.1, f32[256,128]{1,0:T(8,128)} %innov_hbm.1, f32[1,128]{1,0:T(1,128)} %bitcast.7, f32[4,256]{1,0:T(4,128)} %scale_hbm.1, ...), custom_call_target="tpu_custom_call" | custom-call | tf_op jit(solution)/shard_map/pallas_call | solution.py:414
  50.6 1.6 %copy.16 = f32[4,64,128]{2,1,0:T(8,128)} copy(f32[4,64,128]{2,1,0:T(8,128)} %get-tuple-element.6) | data formatting | bytes 262144
  52.2 1.6 %copy.17 = f32[4,64,128]{2,1,0:T(8,128)} copy(f32[4,64,128]{2,1,0:T(8,128)} %get-tuple-element.7) | data formatting | bytes 262144
  53.7 1.4 %copy.18 = f32[8,4,256]{2,1,0:T(4,128)} copy(f32[8,4,256]{2,1,0:T(4,128)} %get-tuple-element.8) | data formatting | bytes 65536
